TPU v7x, 32 devices: a whole 2x2x4 slice. The times are simulated.
32 devices in a mesh: groups: 2 (over y), wide: 4 (over z), narrow: 2 (over x), sub: 2 (over core).
Axes of the slice: x: 2, y: 2, z: 4, core: 2. Of those that a mesh axis runs over, the one named last changes fastest.
Arguments:
- features: bfloat16 [8192, 96], P(('groups', 'wide', 'narrow', 'sub')), parts along dimension 0, may hold values from -6 to 6
- cotangent: bfloat16 [8192, 96], P(('groups', 'wide', 'narrow', 'sub')), parts along dimension 0, may hold values from -6 to 6
- keys: int32 [8192], P(('groups', 'wide', 'narrow', 'sub')), parts along dimension 0, may hold values from 0 to 8191, as said below
- weight: bfloat16 [27, 96, 96], replicated, may hold values from -0.125 to 0.125
Outputs:
- out_rows: bfloat16 [8192, 96], P(('groups', 'wide', 'narrow', 'sub')), parts along dimension 0
- grad_rows: bfloat16 [8192, 96], P(('groups', 'wide', 'narrow', 'sub')), parts along dimension 0
- weight_grad: float32 [497664], P(('groups', 'wide', 'narrow', 'sub')), parts along dimension 0
There are 2 independent parts, one for each index of `groups`. A program takes and returns all parts, laid end to end along the dimension named above; an argument that names none is the same for every part. Nothing has to cross between parts.
Inputs may be any that keep to these rules, and one draw needn't show every extreme that they name: Keys are distinct and ascend on each device; key // 512 names a brick piece whose sub index equals the holding device's sub index; one device holds at most 64 keys of one brick piece, and for each sub index one brick piece gets exactly 64 keys from every device of that sub index.
All inputs are finite; a program needn't handle non-finite values.
Results may differ from a plain program's by a relative error of at most 0.001.
Values may be sent and summed in bfloat16 or wider, within the bound.
A program may use at most 64 MiB of HBM per device.

v0:
```python
import jax
import jax.numpy as jnp
from jax import lax
from jax.sharding import PartitionSpec as P

EDGE = 16
DEPTH = 4


def extended(array, sides, width):
    for axis, dim in sides:
        size, length = (lax.axis_size(axis), array.shape[dim])
        up = [(i, (i + 1) % size) for i in range(size - 1)]
        down = [(j, i) for i, j in up]
        last = lax.slice_in_dim(array, length - width, length, axis=dim)
        first = lax.slice_in_dim(array, 0, width, axis=dim)
        before = lax.ppermute(last, axis, up)
        after = lax.ppermute(first, axis, down)
        array = jnp.concatenate([before, array, after], axis=dim)
    return array


def brick_pass(padded, weight, chan_count, half_depth):
    fields = padded[..., :chan_count]
    back_field = padded[..., chan_count:]
    centre = back_field[1:-1, 1:-1, 1:-1].reshape(-1, chan_count)
    cell_count = EDGE * EDGE * half_depth
    forward = jnp.zeros((cell_count, chan_count), jnp.float32)
    backward = jnp.zeros((cell_count, chan_count), jnp.float32)
    pieces = []
    for group in range(9):
        step_x = group // 3 - 1
        step_y = group % 3 - 1
        shifted = jnp.concatenate(
            [
                fields[
                    1 + step_x : 1 + step_x + EDGE,
                    1 + step_y : 1 + step_y + EDGE,
                    1 + step_z : 1 + step_z + half_depth,
                ]
                for step_z in (-1, 0, 1)
            ],
            axis=3,
        ).reshape(-1, 3 * chan_count)
        mirrored = jnp.concatenate(
            [
                back_field[
                    1 - step_x : 1 - step_x + EDGE,
                    1 - step_y : 1 - step_y + EDGE,
                    1 - step_z : 1 - step_z + half_depth,
                ]
                for step_z in (-1, 0, 1)
            ],
            axis=3,
        ).reshape(-1, 3 * chan_count)
        tap_block = weight[3 * group : 3 * group + 3]
        forward = forward + jnp.dot(
            shifted,
            tap_block.reshape(3 * chan_count, chan_count),
            preferred_element_type=jnp.float32,
        )
        backward = backward + jnp.dot(
            mirrored,
            jnp.transpose(tap_block, (0, 2, 1)).reshape(3 * chan_count, chan_count),
            preferred_element_type=jnp.float32,
        )
        pieces.append(
            lax.dot_general(
                shifted, centre, (((0,), (0,)), ((), ())), preferred_element_type=jnp.float32
            )
        )
    weight_terms = jnp.concatenate(pieces, axis=0)
    return (forward.astype(jnp.bfloat16), backward.astype(jnp.bfloat16), weight_terms)


def shards(features, cotangent, keys, weight):
    row_count, chan_count = features.shape
    wide_size = lax.axis_size("wide")
    narrow = lax.axis_size("narrow")
    sub_size = lax.axis_size("sub")
    owners = wide_size * narrow
    capacity = 2 * row_count // owners
    slot_count = owners * capacity
    half_depth = DEPTH // sub_size
    cell_count = EDGE * EDGE * half_depth
    target = keys // cell_count // sub_size
    local_cell = keys % cell_count
    columns = jnp.arange(owners, dtype=jnp.int32)
    before = jnp.sum((target[:, None] < columns[None, :]).astype(jnp.int32), axis=0)
    matches = target[:, None] == columns[None, :]
    first_row = jnp.sum(jnp.where(matches, before[None, :], 0), axis=1)
    row_rank = jnp.arange(row_count, dtype=jnp.int32) - first_row
    send_slot = target * capacity + row_rank
    payload = jnp.concatenate([features, cotangent], axis=1)
    outgoing = jnp.zeros((slot_count, 2 * chan_count), jnp.bfloat16).at[send_slot].set(payload)
    placed = jnp.full((slot_count,), -1, jnp.int32).at[send_slot].set(local_cell)
    incoming, arrived = (
        lax.all_to_all(outgoing, ("wide", "narrow"), split_axis=0, concat_axis=0, tiled=True),
        lax.all_to_all(placed, ("wide", "narrow"), split_axis=0, concat_axis=0, tiled=True),
    )
    is_live = arrived >= 0
    position = jnp.where(is_live, arrived, cell_count)
    dense = jnp.zeros((cell_count + 1, 2 * chan_count), jnp.bfloat16).at[position].set(incoming)
    dense = dense[:cell_count].reshape(EDGE, EDGE, half_depth, 2 * chan_count)
    padded = extended(dense, (("wide", 1), ("narrow", 0), ("sub", 2)), 1)
    outputs, gradient, weight_terms = brick_pass(padded, weight, chan_count, half_depth)
    reply = jnp.concatenate([outputs, gradient], axis=1)
    picked = jnp.where(
        is_live[:, None], reply[jnp.where(is_live, arrived, 0)], jnp.zeros((), jnp.bfloat16)
    )
    returned = lax.all_to_all(picked, ("wide", "narrow"), split_axis=0, concat_axis=0, tiled=True)
    answer = returned[send_slot]
    flat_terms = weight_terms.reshape(-1)
    partial_value = lax.psum_scatter(flat_terms, "wide", scatter_dimension=0, tiled=True)
    summed = lax.psum_scatter(partial_value, ("narrow", "sub"), scatter_dimension=0, tiled=True)
    factor = jnp.float32(1.0) / jnp.sqrt(jnp.float32(row_count * owners * sub_size))
    return (answer[:, :chan_count], answer[:, chan_count:], summed * factor)


def solution(mesh):
    placed = (
        P(("groups", "wide", "narrow", "sub"), None),
        P(("groups", "wide", "narrow", "sub"), None),
        P(("groups", "wide", "narrow", "sub")),
        P(),
    )
    return jax.shard_map(
        shards,
        mesh=mesh,
        in_specs=placed,
        out_specs=(
            P(("groups", "wide", "narrow", "sub"), None),
            P(("groups", "wide", "narrow", "sub"), None),
            P(("groups", "wide", "narrow", "sub")),
        ),
        check_vma=False,
    )
```

profile of v0, /device:TPU:0, one launch (start us, length us, event | category | flops | bytes accessed | tf_op | source)
XLA Modules:
  0.0 216.3 jit_solution(16850231097534099650)
XLA Ops:
  8.1 1.4 scatter_custom_fusion
  10.2 7.3 %all-to-all-start = ((s32[8,64,1]{1,2,0:T(1,128)}), s32[8,64,1]{1,2,0:T(1,128)S(1)}, u32[]{:S(2)}, u32[]{:S(2)}) async-start(s32[8,64,1]{1,2,0:T(1,128)} %all_to_all.22), calls=%async_computation | async-start | bytes 8192 | tf_op jit(solution)/shard_map/all_to_all | solution.py:99
  17.5 2.1 fusion.25
  26.3 2.1 scatter_custom_fusion.1
  28.4 6.0 %all-to-all-start.1 = ((bf16[8,64,192]{2,1,0:T(8,128)(2,1)}), bf16[8,64,192]{2,1,0:T(8,128)(2,1)S(1)}, u32[]{:S(2)}, u32[]{:S(2)}) async-start(bf16[8,64,192]{2,1,0:T(8,128)(2,1)} %bitcast.3), calls=%async_computation.1 | async-start | bytes 524288 | tf_op jit(solution)/shard_map/all_to_all | solution.py:98
  35.7 7.2 %all-to-all-done.1 = bf16[8,64,192]{2,1,0:T(8,128)(2,1)S(1)} async-done(((bf16[8,64,192]{2,1,0:T(8,128)(2,1)}), bf16[8,64,192]{2,1,0:T(8,128)(2,1)S(1)}, u32[]{:S(2)}, u32[]{:S(2)}) %all-to-all-start.1) | async-done | bytes 196640 | tf_op jit(solution)/shard_map/all_to_all | solution.py:98
  42.9 2.4 %scatter_custom_fusion.2 = bf16[513,192]{1,0:T(8,128)(2,1)S(1)} fusion(s32[512]{0:T(512)S(1)} %bitcast.144, bf16[512,192]{1,0:T(8,128)(2,1)S(1)} %bitcast.141, bf16[]{:T(256)} %constant.50.clone.1), kind=kCustom, calls=%fused_computation.66 | custom fusion | bytes 196994 | tf_op jit(solution)/shard_map/scatter | solution.py:103
  46.9 4.5 %collective-permute-start = (bf16[16,1,2,192]{3,1,2,0:T(2,128)(2,1)S(1)}, bf16[16,1,2,192]{3,1,2,0:T(2,128)(2,1)S(1)}, u32[]{:S(2)}, u32[]{:S(2)}) collective-permute-start(bf16[16,1,2,192]{3,1,2,0:T(2,128)(2,1)S(1)} %get-tuple-element.103), channel_id=1, source_target_pairs={{0,4},{4,8},{8,12},{1,5},{5,9},{9,13},{2,6},{6,10},{10,14},{3,7},{... | collective-permute-start | bytes 36872 | tf_op jit(solution)/shard_map/ppermute | solution.py:17
  54.3 4.5 %collective-permute-start.2 = (bf16[1,18,2,192]{3,1,2,0:T(8,128)(2,1)S(1)}, bf16[1,18,2,192]{3,1,2,0:T(8,128)(2,1)S(1)}, u32[]{:S(2)}, u32[]{:S(2)}) collective-permute-start(bf16[1,18,2,192]{3,1,2,0:T(8,128)(2,1)S(1)} %get-tuple-element.95), channel_id=1, source_target_pairs={{0,2},{1,3},{4,6},{5,7},{8,10},{9,11},{12,14},{13,15},{16,18},{17,... | collective-permute-start | bytes 41480 | tf_op jit(solution)/shard_map/ppermute | solution.py:17
  62.0 3.2 %collective-permute-start.4 = (bf16[18,18,1,192]{3,1,2,0:T(8,128)(2,1)S(1)}, bf16[18,18,1,192]{3,1,2,0:T(8,128)(2,1)S(1)}, u32[]{:S(2)}, u32[]{:S(2)}) collective-permute-start(bf16[18,18,1,192]{3,1,2,0:T(8,128)(2,1)S(1)} %get-tuple-element.76), channel_id=1, source_target_pairs={{0,1},{2,3},{4,5},{6,7},{8,9},{10,11},{12,13},{14,15},{16,17},{18,... | collective-permute-start | bytes 373256 | tf_op jit(solution)/shard_map/ppermute | solution.py:17
  68.0 1.4 fusion.27
  69.4 1.4 fusion.26
  86.5 1.6 pad_maximum_fusion.12
  90.9 1.6 pad_maximum_fusion.14
  96.9 1.6 pad_maximum_fusion.16
  113.1 1.8 concatenate.162
  115.4 1.8 reshape.227
  124.5 2.0 gather_fusion
  127.3 5.7 %all-to-all-start.2 = ((bf16[8,64,192]{2,1,0:T(8,128)(2,1)}), bf16[8,64,192]{2,1,0:T(8,128)(2,1)S(1)}, u32[]{:S(2)}, u32[]{:S(2)}) async-start(bf16[8,64,192]{2,1,0:T(8,128)(2,1)} %broadcast_select_fusion), calls=%async_computation.2 | async-start | bytes 524288 | tf_op jit(solution)/shard_map/all_to_all | solution.py:111
  135.6 13.2 %all-to-all-done.2 = bf16[8,64,192]{2,1,0:T(8,128)(2,1)S(1)} async-done(((bf16[8,64,192]{2,1,0:T(8,128)(2,1)}), bf16[8,64,192]{2,1,0:T(8,128)(2,1)S(1)}, u32[]{:S(2)}, u32[]{:S(2)}) %all-to-all-start.2) | async-done | bytes 196640 | tf_op jit(solution)/shard_map/all_to_all | solution.py:111
  149.9 24.5 %all-reduce.5.cloned.1.call-done = f32[248832]{0:T(1024)} async-done(((f32[248832]{0:T(1024)}), f32[248832]{0:T(1024)}) %all-reduce.5.cloned.1.call-update) | async-done | bytes 995344
  174.5 1.8 dynamic-slice.1
  177.9 30.0 %all-reduce.7.cloned.1.call-done = f32[62208]{0:T(1024)} async-done(((f32[62208]{0:T(1024)}), f32[62208]{0:T(1024)}) %all-reduce.7.cloned.1.call-update) | async-done | bytes 248848
  207.9 1.6 dynamic-slice_multiply_fusion
  (224 shorter events, 69.4 us)
Async XLA Ops:
  7.2 12.4 %copy-start.43 = (bf16[256,96]{0,1:T(8,128)(2,1)S(1)}, bf16[256,96]{0,1:T(8,128)(2,1)}, u32[]{:S(2)}) copy-start(bf16[256,96]{0,1:T(8,128)(2,1)} %param.5) | copy-start | bytes 147460
  7.2 12.4 %copy-start.44 = (bf16[256,96]{0,1:T(8,128)(2,1)S(1)}, bf16[256,96]{0,1:T(8,128)(2,1)}, u32[]{:S(2)}) copy-start(bf16[256,96]{0,1:T(8,128)(2,1)} %param.4) | copy-start | bytes 147460
  10.2 18.2 %all-to-all-start = ((s32[8,64,1]{1,2,0:T(1,128)}), s32[8,64,1]{1,2,0:T(1,128)S(1)}, u32[]{:S(2)}, u32[]{:S(2)}) async-start(s32[8,64,1]{1,2,0:T(1,128)} %all_to_all.22), calls=%async_computation | async-start | bytes 8192 | tf_op jit(solution)/shard_map/all_to_all | solution.py:99
  28.4 14.5 %all-to-all-start.1 = ((bf16[8,64,192]{2,1,0:T(8,128)(2,1)}), bf16[8,64,192]{2,1,0:T(8,128)(2,1)S(1)}, u32[]{:S(2)}, u32[]{:S(2)}) async-start(bf16[8,64,192]{2,1,0:T(8,128)(2,1)} %bitcast.3), calls=%async_computation.1 | async-start | bytes 524288 | tf_op jit(solution)/shard_map/all_to_all | solution.py:98
  34.4 140.1 %all-reduce.5.cloned.1.call-start = ((), (), s32[]{:S(2)}) async-start(), calls=%async_computation.3 | async-start | bytes 1990656
  45.6 6.6 %collective-permute-start.1 = (bf16[16,1,2,192]{3,1,2,0:T(2,128)(2,1)S(1)}, bf16[16,1,2,192]{3,1,2,0:T(2,128)(2,1)S(1)}, u32[]{:S(2)}, u32[]{:S(2)}) collective-permute-start(bf16[16,1,2,192]{3,1,2,0:T(2,128)(2,1)S(1)} %get-tuple-element.104), channel_id=1, source_target_pairs={{4,0},{8,4},{12,8},{5,1},{9,5},{13,9},{6,2},{10,6},{14,10},{7,3},{... | collective-permute-start | bytes 36872 | tf_op jit(solution)/shard_map/ppermute | solution.py:18
  46.9 6.1 %collective-permute-start = (bf16[16,1,2,192]{3,1,2,0:T(2,128)(2,1)S(1)}, bf16[16,1,2,192]{3,1,2,0:T(2,128)(2,1)S(1)}, u32[]{:S(2)}, u32[]{:S(2)}) collective-permute-start(bf16[16,1,2,192]{3,1,2,0:T(2,128)(2,1)S(1)} %get-tuple-element.103), channel_id=1, source_target_pairs={{0,4},{4,8},{8,12},{1,5},{5,9},{9,13},{2,6},{6,10},{10,14},{3,7},{... | collective-permute-start | bytes 36872 | tf_op jit(solution)/shard_map/ppermute | solution.py:17
  53.0 6.7 %collective-permute-start.3 = (bf16[1,18,2,192]{3,1,2,0:T(8,128)(2,1)S(1)}, bf16[1,18,2,192]{3,1,2,0:T(8,128)(2,1)S(1)}, u32[]{:S(2)}, u32[]{:S(2)}) collective-permute-start(bf16[1,18,2,192]{3,1,2,0:T(8,128)(2,1)S(1)} %get-tuple-element.96), channel_id=1, source_target_pairs={{2,0},{3,1},{6,4},{7,5},{10,8},{11,9},{14,12},{15,13},{18,16},{19,... | collective-permute-start | bytes 41480 | tf_op jit(solution)/shard_map/ppermute | solution.py:18
  54.3 6.1 %collective-permute-start.2 = (bf16[1,18,2,192]{3,1,2,0:T(8,128)(2,1)S(1)}, bf16[1,18,2,192]{3,1,2,0:T(8,128)(2,1)S(1)}, u32[]{:S(2)}, u32[]{:S(2)}) collective-permute-start(bf16[1,18,2,192]{3,1,2,0:T(8,128)(2,1)S(1)} %get-tuple-element.95), channel_id=1, source_target_pairs={{0,2},{1,3},{4,6},{5,7},{8,10},{9,11},{12,14},{13,15},{16,18},{17,... | collective-permute-start | bytes 41480 | tf_op jit(solution)/shard_map/ppermute | solution.py:17
  60.7 6.8 %collective-permute-start.5 = (bf16[18,18,1,192]{3,1,2,0:T(8,128)(2,1)S(1)}, bf16[18,18,1,192]{3,1,2,0:T(8,128)(2,1)S(1)}, u32[]{:S(2)}, u32[]{:S(2)}) collective-permute-start(bf16[18,18,1,192]{3,1,2,0:T(8,128)(2,1)S(1)} %get-tuple-element.75), channel_id=1, source_target_pairs={{1,0},{3,2},{5,4},{7,6},{9,8},{11,10},{13,12},{15,14},{17,16},{19,... | collective-permute-start | bytes 373256 | tf_op jit(solution)/shard_map/ppermute | solution.py:18
  62.0 5.5 %collective-permute-start.4 = (bf16[18,18,1,192]{3,1,2,0:T(8,128)(2,1)S(1)}, bf16[18,18,1,192]{3,1,2,0:T(8,128)(2,1)S(1)}, u32[]{:S(2)}, u32[]{:S(2)}) collective-permute-start(bf16[18,18,1,192]{3,1,2,0:T(8,128)(2,1)S(1)} %get-tuple-element.76), channel_id=1, source_target_pairs={{0,1},{2,3},{4,5},{6,7},{8,9},{10,11},{12,13},{14,15},{16,17},{18,... | collective-permute-start | bytes 373256 | tf_op jit(solution)/shard_map/ppermute | solution.py:17
  98.9 2.5 %copy-start.20 = (bf16[16,16,2,96]{3,1,2,0:T(8,128)(2,1)S(1)}, bf16[16,16,2,96]{3,1,2,0:T(8,128)(2,1)}, u32[]{:S(2)}) copy-start(bf16[16,16,2,96]{3,1,2,0:T(8,128)(2,1)} %get-tuple-element.84) | copy-start | bytes 294916
  98.9 2.5 %copy-start.21 = (bf16[16,16,2,96]{3,1,2,0:T(8,128)(2,1)S(1)}, bf16[16,16,2,96]{3,1,2,0:T(8,128)(2,1)}, u32[]{:S(2)}) copy-start(bf16[16,16,2,96]{3,1,2,0:T(8,128)(2,1)} %get-tuple-element.58) | copy-start | bytes 294916
  98.9 2.5 %copy-start.22 = (bf16[16,16,2,96]{3,1,2,0:T(8,128)(2,1)S(1)}, bf16[16,16,2,96]{3,1,2,0:T(8,128)(2,1)}, u32[]{:S(2)}) copy-start(bf16[16,16,2,96]{3,1,2,0:T(8,128)(2,1)} %get-tuple-element.40) | copy-start | bytes 294916
  106.4 2.5 %copy-start = (bf16[16,16,2,288]{3,1,2,0:T(8,128)(2,1)S(1)}, bf16[16,16,2,288]{3,1,2,0:T(8,128)(2,1)}, u32[]{:S(2)}) copy-start(bf16[16,16,2,288]{3,1,2,0:T(8,128)(2,1)} %get-tuple-element.115) | copy-start | bytes 884740
  107.8 2.5 %copy-start.4 = (bf16[16,16,2,288]{3,1,2,0:T(8,128)(2,1)S(1)}, bf16[16,16,2,288]{3,1,2,0:T(8,128)(2,1)}, u32[]{:S(2)}) copy-start(bf16[16,16,2,288]{3,1,2,0:T(8,128)(2,1)} %get-tuple-element.116) | copy-start | bytes 884740
  109.2 2.5 %copy-start.1 = (bf16[16,16,2,288]{3,1,2,0:T(8,128)(2,1)S(1)}, bf16[16,16,2,288]{3,1,2,0:T(8,128)(2,1)}, u32[]{:S(2)}) copy-start(bf16[16,16,2,288]{3,1,2,0:T(8,128)(2,1)} %get-tuple-element.117) | copy-start | bytes 884740
  110.6 2.5 %copy-start.19 = (f32[288,96]{0,1:T(8,128)S(1)}, f32[288,96]{0,1:T(8,128)}, u32[]{:S(2)}) copy-start(f32[288,96]{0,1:T(8,128)} %convolution_bitcast_fusion.5) | copy-start | bytes 331780
  110.6 2.5 %copy-start.41 = (f32[288,96]{0,1:T(8,128)S(1)}, f32[288,96]{0,1:T(8,128)}, u32[]{:S(2)}) copy-start(f32[288,96]{0,1:T(8,128)} %convolution_bitcast_fusion.7) | copy-start | bytes 331780
  110.6 2.5 %copy-start.42 = (f32[288,96]{0,1:T(8,128)S(1)}, f32[288,96]{0,1:T(8,128)}, u32[]{:S(2)}) copy-start(f32[288,96]{0,1:T(8,128)} %convolution_bitcast_fusion.6) | copy-start | bytes 331780
  124.4 8.6 %copy-start.46 = (u32[32]{0:T(128)S(1)}, u32[32]{0:T(128)}, u32[]{:S(2)}) copy-start(u32[32]{0:T(128)} %constant.55) | copy-start | bytes 388
  124.4 9.2 %copy-start.45 = (u32[32]{0:T(128)S(1)}, u32[32]{0:T(128)}, u32[]{:S(2)}) copy-start(u32[32]{0:T(128)} %constant.59) | copy-start | bytes 388
  127.3 21.5 %all-to-all-start.2 = ((bf16[8,64,192]{2,1,0:T(8,128)(2,1)}), bf16[8,64,192]{2,1,0:T(8,128)(2,1)S(1)}, u32[]{:S(2)}, u32[]{:S(2)}) async-start(bf16[8,64,192]{2,1,0:T(8,128)(2,1)} %broadcast_select_fusion), calls=%async_computation.2 | async-start | bytes 524288 | tf_op jit(solution)/shard_map/all_to_all | solution.py:111
  133.0 74.9 %all-reduce.7.cloned.1.call-start = ((), (), s32[]{:S(2)}) async-start(), calls=%async_computation.4 | async-start | bytes 499712
  (34 other events, 40.8 us)
Sparse Core Ops, SparseCore 0:
  117.3 57.1 all-reduce.4
  176.9 30.9 all-reduce.6
where the time goes:
time: 217 us; the launch traced here: 216 us
  waiting for transfers between devices  76.4 us (35%)
  local copies, waits for them, and re-layouts  58.7 us (27%)
  starting transfers between devices  35.3 us (16%)
  between operations  16.2 us (7%)
  matrix products  15.2 us (7%)
  other arithmetic  14.6 us (7%)
    unnamed x4, waiting for transfers between devices  54.6 us
    all_to_all x1, waiting for transfers between devices, shards(): lax.all_to_all(picked, ('wide', 'narrow'), split_axis=0, concat_axis=0, t...  13.2 us
    ppermute x3, starting transfers between devices, extended(): before = lax.ppermute(last, axis, up)  12.3 us
    dot_general x9, matrix products, brick_pass(): lax.dot_general(shifted, centre, (((0,), (0,)), ((), ())), preferred_elem...  10.5 us
    reshape x9, local copies, waits for them, and re-layouts, brick_pass(): shifted = jnp.concatenate([fields[1 + step_x:1 + step_x + EDGE, 1 + step_...  8.99 us
    reshape x9, local copies, waits for them, and re-layouts, brick_pass(): mirrored = jnp.concatenate([back_field[1 - step_x:1 - step_x + EDGE, 1 -...  8.22 us
    all_to_all x1, starting transfers between devices, shards(): lax.all_to_all(placed, ('wide', 'narrow'), split_axis=0, concat_axis=0, t...  7.25 us
    all_to_all x1, waiting for transfers between devices, shards(): lax.all_to_all(outgoing, ('wide', 'narrow'), split_axis=0, concat_axis=0,...  7.17 us
  transfers between devices with their start and end apart: 11, of which 6 were waited for; matrix products, arithmetic and copies ran while one was open for 13% of the time, Pallas kernels for 0%

commit v1 on v0

--- a/solution.py
+++ b/solution.py
@@ -1,10 +1,383 @@
+import functools
+
 import jax
 import jax.numpy as jnp
 from jax import lax
+from jax.experimental import pallas as pl
+from jax.experimental.pallas import tpu as pltpu
 from jax.sharding import PartitionSpec as P
 
 EDGE = 16
 DEPTH = 4
+LANES = 128
+F32, BF16 = jnp.float32, jnp.bfloat16
+
+
+def window_kernel(
+    dims, feat_ref, cot_ref, keys_ref, weight_ref, out_ref, grad_ref, wgrad_ref,
+    held, slots, x_field, g_field, x_near, g_near, taps, mask, forward, backward,
+    picked, returned, terms, send_sem, recv_sem, reply_send, reply_recv,
+):
+    wide_n, narrow_n, sub_n, rows, chan, cap, shard = dims
+    owners = wide_n * narrow_n
+    slot_n = owners * cap
+    half = DEPTH // sub_n
+    cells = EDGE * EDGE * half
+    w, n, s = lax.axis_index("wide"), lax.axis_index("narrow"), lax.axis_index("sub")
+    me = w * narrow_n + n
+
+    def number(wi, ni, si):
+        return (wi * narrow_n + ni) * sub_n + si
+
+    def place(wi, ni, si):
+        return {"wide": wi, "narrow": ni, "sub": si}
+
+    barrier = pltpu.get_barrier_semaphore()
+    for delta in range(1, owners):
+        peer = lax.rem(me + delta, owners)
+        pl.semaphore_signal(
+            barrier, inc=1, device_id=place(peer // narrow_n, peer % narrow_n, s),
+            device_id_type=pl.DeviceIdType.MESH,
+        )
+    pl.semaphore_signal(
+        barrier, inc=1, device_id=place(w, n, 1 - s), device_id_type=pl.DeviceIdType.MESH
+    )
+
+    keys = keys_ref[...]
+    target = lax.shift_right_logical(keys, (cells * sub_n).bit_length() - 1)
+    local = keys & (cells - 1)
+    cell = (local >> 5) * 32 + (local & 1) * EDGE + ((local >> 1) & (EDGE - 1))
+    first = jnp.zeros_like(keys)
+    for o in range(1, owners):
+        before = jnp.sum((target < o).astype(F32), axis=1, keepdims=True).astype(jnp.int32)
+        first = jnp.where(target == o, before, first)
+    slot = target * cap + lax.broadcasted_iota(jnp.int32, keys.shape, 1) - first
+    cell1 = cell + 1
+    line = lax.broadcasted_iota(jnp.int32, (LANES, rows), 0)
+    digits = jnp.where(line == 0, slot >> 4, 0)
+    digits = jnp.where(line == 1, slot & 15, digits)
+    digits = jnp.where(line == chan, cell1 >> 4, digits)
+    digits = jnp.where(line == chan + 1, cell1 & 15, digits)
+    digits = digits.astype(F32).astype(BF16)
+    eye = (
+        lax.broadcasted_iota(jnp.int32, (rows, rows), 0)
+        == lax.broadcasted_iota(jnp.int32, (rows, rows), 1)
+    )
+    eye = jnp.where(eye, 1.0, 0.0).astype(BF16)
+    column = lax.dot_general(eye, digits, (((1,), (1,)), ((), ())), preferred_element_type=F32)
+    mine = number(w, n, s)
+    held[mine, 0:rows, 0:LANES] = column.astype(BF16)
+    held[mine, 0:rows, LANES : 2 * LANES] = jnp.zeros((rows, LANES), BF16)
+    held[mine, 0:rows, 0:chan] = feat_ref[...]
+    held[mine, 0:rows, LANES : LANES + chan] = cot_ref[...]
+    held[mine, rows : rows + 16, :] = digits[0:16]
+
+    pl.semaphore_wait(barrier, owners)
+
+    def block_copy(block, kind, target_place):
+        return pltpu.make_async_remote_copy(
+            src_ref=held.at[block], dst_ref=held.at[block],
+            send_sem=send_sem.at[block, kind], recv_sem=recv_sem.at[block],
+            device_id=target_place, device_id_type=pl.DeviceIdType.MESH,
+        )
+
+    up, down = place(w + 1, n, s), place(w - 1, n, s)
+    across, sibling = place(w, 1 - n, s), place(w, n, 1 - s)
+
+    @pl.when(w + 1 < wide_n)
+    def _():
+        block_copy(mine, 0, up).start()
+
+    @pl.when(w >= 1)
+    def _():
+        block_copy(mine, 1, down).start()
+
+    block_copy(mine, 2, across).start()
+    block_copy(mine, 3, sibling).start()
+
+    def clear(i, carry):
+        x_field[i] = jnp.zeros(x_field.shape[1:], F32)
+        g_field[i] = jnp.zeros(g_field.shape[1:], F32)
+        return carry
+
+    lax.fori_loop(0, x_field.shape[0], clear, 0)
+    taps[...] = jnp.zeros(taps.shape, BF16)
+    for t in range(27):
+        taps[t, 0:chan, 0:chan] = weight_ref[t]
+
+    def crossed(distance):
+        def arrive(wi):
+            block = number(wi, 1 - n, s)
+            block_copy(block, 2, across).wait_recv()
+            block_copy(block, 3, sibling).start()
+
+        if distance == 0:
+            arrive(w)
+            return
+
+        @pl.when(w >= distance)
+        def _():
+            arrive(w - distance)
+
+        @pl.when(w + distance < wide_n)
+        def _():
+            arrive(w + distance)
+
+    for d in range(1, wide_n):
+
+        @pl.when(w >= d)
+        def _():
+            block = number(w - d, n, s)
+            block_copy(block, 0, up).wait_recv()
+
+            @pl.when(w + 1 < wide_n)
+            def _():
+                block_copy(block, 0, up).start()
+
+            block_copy(block, 2, across).start()
+            block_copy(block, 3, sibling).start()
+
+        @pl.when(w + d < wide_n)
+        def _():
+            block = number(w + d, n, s)
+            block_copy(block, 1, down).wait_recv()
+
+            @pl.when(w >= 1)
+            def _():
+                block_copy(block, 1, down).start()
+
+            block_copy(block, 2, across).start()
+            block_copy(block, 3, sibling).start()
+
+        crossed(d - 1)
+    crossed(wide_n - 1)
+
+    for o in range(owners):
+        block_copy(o * sub_n + 1 - s, 3, sibling).wait_recv()
+
+    for wi in range(wide_n):
+        block = number(wi, n, s)
+
+        @pl.when(jnp.logical_and(wi <= w, w + 1 < wide_n))
+        def _():
+            block_copy(block, 0, up).wait_send()
+
+        @pl.when(jnp.logical_and(wi >= w, w >= 1))
+        def _():
+            block_copy(block, 1, down).wait_send()
+
+        block_copy(block, 2, across).wait_send()
+        for ni in range(narrow_n):
+            block_copy(number(wi, ni, s), 3, sibling).wait_send()
+
+    def slot_mask(block):
+        lines = held[block, rows : rows + 16, :].astype(F32)
+        slot_of = lines[0:1] * 16.0 + lines[1:2]
+        order = lax.broadcasted_iota(jnp.int32, (slot_n, rows), 0).astype(F32)
+        return jnp.where(order == slot_of, 1.0, 0.0).astype(BF16)
+
+    def to_slots(block, carry):
+        filled = jnp.dot(slot_mask(block), held[block, 0:rows, :], preferred_element_type=F32)
+        source = block // sub_n
+        slots[block % sub_n, :, source] = filled.astype(BF16).reshape(owners, cap, 2 * LANES)
+        return carry
+
+    lax.fori_loop(0, owners * sub_n, to_slots, 0)
+
+    row_of = lax.broadcasted_iota(jnp.int32, (16, 2 * LANES), 0)
+    lane_of = lax.broadcasted_iota(jnp.int32, (16, 2 * LANES), 1)
+    chooser = jnp.where(lane_of == chan, 16.0, jnp.where(lane_of == chan + 1, 1.0, 0.0))
+    chooser = jnp.where(row_of == 0, chooser, 0.0).astype(BF16)
+
+    def cell_mask(block):
+        rows_in = slots[block % sub_n, block // sub_n].reshape(slot_n, 2 * LANES)
+        cell_of = lax.dot_general(
+            chooser, rows_in, (((1,), (1,)), ((), ())), preferred_element_type=F32
+        )[0:1]
+        order = lax.broadcasted_iota(jnp.int32, (cells, slot_n), 0).astype(F32) + 1.0
+        return jnp.where(order == cell_of, 1.0, 0.0).astype(BF16), rows_in
+
+    def to_field(block, carry):
+        ones, rows_in = cell_mask(block)
+        dense = jnp.dot(ones, rows_in, preferred_element_type=F32)
+        dense = dense.reshape(EDGE, half, EDGE, 2 * LANES)
+        owner = block // sub_n
+        at = (
+            pl.ds(1 + EDGE * (owner % narrow_n), EDGE),
+            pl.ds(1 + half * (block % sub_n), half),
+            pl.ds(pl.multiple_of(EDGE + EDGE * (owner // narrow_n), EDGE), EDGE),
+        )
+        x_field[at] = dense[..., 0:LANES]
+        g_field[at] = dense[..., LANES : 2 * LANES]
+        return carry
+
+    lax.fori_loop(0, owners * sub_n, to_field, 0)
+    mask[...] = cell_mask(mine)[0]
+
+    wide_at = pl.ds(pl.multiple_of(EDGE * w, EDGE), 3 * EDGE)
+
+    def near(i, carry):
+        for k in range(half + 2):
+            x_line = x_field[EDGE * n + i, half * s + k, wide_at, :]
+            g_line = g_field[EDGE * n + i, half * s + k, wide_at, :]
+            for j in range(3):
+                begin = EDGE - 1 + j
+                x_near[j, i, k] = x_line[begin : begin + EDGE].astype(BF16)
+                g_near[j, i, k] = g_line[begin : begin + EDGE].astype(BF16)
+        return carry
+
+    lax.fori_loop(0, EDGE + 2, near, 0)
+
+    forward[...] = jnp.zeros(forward.shape, F32)
+    backward[...] = jnp.zeros(backward.shape, F32)
+
+    def conv(group, carry):
+        i, j = group // 3, group % 3
+        ahead = jnp.concatenate(
+            [x_near[j, pl.ds(i, EDGE), k : k + half].reshape(cells, LANES) for k in range(3)],
+            axis=1,
+        )
+        behind = [
+            g_near[2 - j, pl.ds(2 - i, EDGE), 2 - k : 2 - k + half].reshape(cells, LANES)
+            for k in range(3)
+        ]
+        forward[...] += jnp.dot(
+            ahead, taps[pl.ds(3 * group, 3)].reshape(3 * LANES, LANES), preferred_element_type=F32
+        )
+        total = backward[...]
+        for k in range(3):
+            total += lax.dot_general(
+                behind[k], taps[3 * group + k], (((1,), (1,)), ((), ())),
+                preferred_element_type=F32,
+            )
+        backward[...] = total
+        return carry
+
+    lax.fori_loop(0, 9, conv, 0)
+
+    reply = jnp.concatenate([forward[...].astype(BF16), backward[...].astype(BF16)], axis=1)
+    rows_out = lax.dot_general(
+        mask[...], reply, (((0,), (0,)), ((), ())), preferred_element_type=F32
+    ).astype(BF16)
+    picked[...] = rows_out.reshape(owners, cap, 2 * LANES)
+
+    def reply_copy(delta):
+        peer = lax.rem(me + delta, owners)
+        return pltpu.make_async_remote_copy(
+            src_ref=picked.at[peer], dst_ref=returned.at[me],
+            send_sem=reply_send.at[delta], recv_sem=reply_recv.at[delta],
+            device_id=place(peer // narrow_n, peer % narrow_n, s),
+            device_id_type=pl.DeviceIdType.MESH,
+        )
+
+    def reply_arrival(delta):
+        peer = lax.rem(me + owners - delta, owners)
+        return pltpu.make_async_remote_copy(
+            src_ref=picked.at[peer], dst_ref=returned.at[peer],
+            send_sem=reply_send.at[delta], recv_sem=reply_recv.at[delta],
+            device_id=place(peer // narrow_n, peer % narrow_n, s),
+            device_id_type=pl.DeviceIdType.MESH,
+        )
+
+    for delta in range(1, owners):
+        reply_copy(delta).start()
+    returned[me] = picked[me]
+
+    begin = mine * shard
+    tap0 = begin // chan
+    whole = EDGE * wide_n
+    terms[...] = jnp.zeros(terms.shape, F32)
+    steps = []
+    for m in range(3):
+        t = jnp.minimum(tap0 + m, 26)
+        steps.append((t // 9, t // 3 % 3, t % 3))
+
+    def gather(i, carry):
+        right = []
+        for a, b, c in steps:
+            right.append(
+                jnp.concatenate(
+                    [
+                        x_field[i + a, c + k, pl.ds(EDGE - 1 + b, whole), :].astype(BF16)
+                        for k in range(DEPTH)
+                    ],
+                    axis=0,
+                )
+            )
+        left = jnp.concatenate(
+            [g_field[1 + i, 1 + k, EDGE : EDGE + whole, :].astype(BF16) for k in range(DEPTH)],
+            axis=0,
+        )
+        terms[...] += lax.dot_general(
+            left, jnp.concatenate(right, axis=1), (((0,), (0,)), ((), ())),
+            preferred_element_type=F32,
+        )
+        return carry
+
+    lax.fori_loop(0, EDGE * narrow_n, gather, 0)
+    total_rows = rows * owners * sub_n
+    factor = F32(1.0) / jnp.sqrt(F32(total_rows))
+    for m in range(3):
+        flipped = jnp.transpose(terms[:, m * LANES : (m + 1) * LANES])
+        forward[m * chan : (m + 1) * chan, :] = flipped[0:chan] * factor
+    wgrad_ref[...] = forward[pl.ds(begin - tap0 * chan, shard), :][:, 0:chan]
+
+    for delta in range(1, owners):
+        reply_copy(delta).wait_send()
+        reply_arrival(delta).wait_recv()
+    answer = lax.dot_general(
+        slot_mask(mine), returned[...].reshape(slot_n, 2 * LANES), (((0,), (0,)), ((), ())),
+        preferred_element_type=F32,
+    ).astype(BF16)
+    out_ref[...] = answer[:, 0:chan]
+    grad_ref[...] = answer[:, LANES : LANES + chan]
+
+
+def window_shards(features, cotangent, keys, weight):
+    rows, chan = features.shape
+    wide_n, narrow_n, sub_n = (lax.axis_size(a) for a in ("wide", "narrow", "sub"))
+    owners = wide_n * narrow_n
+    cap = 2 * rows // owners
+    half = DEPTH // sub_n
+    cells = EDGE * EDGE * half
+    shard = 27 * chan // (owners * sub_n)
+    field = (EDGE * narrow_n + 2, DEPTH + 2, EDGE * wide_n + 2 * EDGE, LANES)
+    near = (3, EDGE + 2, half + 2, EDGE, LANES)
+    dims = (wide_n, narrow_n, sub_n, rows, chan, cap, shard)
+    vmem = pl.BlockSpec(memory_space=pltpu.VMEM)
+    out, grad, terms = pl.pallas_call(
+        functools.partial(window_kernel, dims),
+        out_shape=(
+            jax.ShapeDtypeStruct((rows, chan), BF16),
+            jax.ShapeDtypeStruct((rows, chan), BF16),
+            jax.ShapeDtypeStruct((shard, chan), F32),
+        ),
+        in_specs=[vmem] * 4,
+        out_specs=(vmem,) * 3,
+        scratch_shapes=[
+            pltpu.VMEM((owners * sub_n, rows + 16, 2 * LANES), BF16),
+            pltpu.VMEM((sub_n, owners, owners, cap, 2 * LANES), BF16),
+            pltpu.VMEM(field, F32),
+            pltpu.VMEM(field, F32),
+            pltpu.VMEM(near, BF16),
+            pltpu.VMEM(near, BF16),
+            pltpu.VMEM((27, LANES, LANES), BF16),
+            pltpu.VMEM((cells, owners * cap), BF16),
+            pltpu.VMEM((cells, LANES), F32),
+            pltpu.VMEM((cells, LANES), F32),
+            pltpu.VMEM((owners, cap, 2 * LANES), BF16),
+            pltpu.VMEM((owners, cap, 2 * LANES), BF16),
+            pltpu.VMEM((LANES, 3 * LANES), F32),
+            pltpu.SemaphoreType.DMA((owners * sub_n, 4)),
+            pltpu.SemaphoreType.DMA((owners * sub_n,)),
+            pltpu.SemaphoreType.DMA((owners,)),
+            pltpu.SemaphoreType.DMA((owners,)),
+        ],
+        compiler_params=pltpu.CompilerParams(
+            collective_id=0, has_side_effects=True, vmem_limit_bytes=50 * 1024 * 1024
+        ),
+    )(features, cotangent, keys.reshape(1, rows), weight)
+    return out, grad, terms.reshape(-1)
 
 
 def extended(array, sides, width):
@@ -124,8 +497,10 @@
         P(("groups", "wide", "narrow", "sub")),
         P(),
     )
+    sizes = mesh.shape
+    gathered = sizes["wide"] * sizes["narrow"] <= 8 and sizes["narrow"] == 2 and sizes["sub"] == 2
     return jax.shard_map(
-        shards,
+        window_shards if gathered else shards,
         mesh=mesh,
         in_specs=placed,
         out_specs=(

time: 217 us -> 52.4 us (0.24)
  waiting for transfers between devices: 76.4 us -> 0 us
  local copies, waits for them, and re-layouts: 58.7 us -> 4.86 us
  Pallas kernels: 0 us -> 46.6 us
  starting transfers between devices: 35.3 us -> 0 us
  between operations: 16.2 us -> 0.68 us
  matrix products: 15.2 us -> 0 us
  other arithmetic: 14.6 us -> 0 us
    unnamed x4 -> x0, waiting for transfers between devices: 54.6 us -> none
    pallas_call x0 -> x1, Pallas kernels: none -> 46.6 us  [window_shards(): pl.pallas_call(functools.partial(window_kernel, dims), out_shape=(jax.Sha...]
    all_to_all x3 -> x0, waiting for transfers between devices: 20.4 us -> none  [the longest x1 13.2 us: shards(): lax.all_to_all(picked, ('wide', 'narrow'), split_axis=0, concat_axis=0, t...]
    all_to_all x3 -> x0, starting transfers between devices: 19 us -> none  [the longest x1 7.25 us: shards(): lax.all_to_all(placed, ('wide', 'narrow'), split_axis=0, concat_axis=0, t...]
    reshape x20 -> x1, local copies, waits for them, and re-layouts: 19.1 us -> 0.73 us  [window_shards(): return (out, grad, terms.reshape(-1))]
    ppermute x6 -> x0, starting transfers between devices: 16.2 us -> none  [the longest x3 12.3 us: extended(): before = lax.ppermute(last, axis, up)]
    dot_general x27 -> x0, matrix products: 15.2 us -> none  [the longest x9 10.5 us: brick_pass(): lax.dot_general(shifted, centre, (((0,), (0,)), ((), ())), preferred_elem...]
    concatenate x14 -> x0, other arithmetic: 10.5 us -> none  [the longest x4 5.05 us: brick_pass(): jnp.concatenate([back_field[1 - step_x:1 - step_x + EDGE, 1 - step_y:1 -...]
  transfers between devices with their start and end apart: 11 -> 0, of which waited for: 6 -> 0; matrix products, arithmetic and copies ran while one was open for 13% -> 0% of each run, Pallas kernels for 0% -> 0%
where the time goes in v1:
time: 52.4 us; the launch traced here: 52.2 us
  Pallas kernels  46.6 us (89%)
  local copies, waits for them, and re-layouts  4.86 us (9%)
  between operations  0.68 us (1%)
    pallas_call x1, Pallas kernels, window_shards(): pl.pallas_call(functools.partial(window_kernel, dims), out_shape=(jax.Sha...  46.6 us
    unnamed x10, local copies, waits for them, and re-layouts  4.13 us

profile of v1, /device:TPU:0, one launch (start us, length us, event | category | flops | bytes accessed | tf_op | source)
XLA Modules:
  0.0 52.2 jit_solution(775052565935569895)
XLA Ops:
  0.6 0.0 copy-start.2
  0.6 0.9 %copy.7.feat_ref = bf16[256,96]{1,0:T(8,128)(2,1)S(1)} copy(bf16[256,96]{0,1:T(8,128)(2,1)} %param.4) | data formatting | bytes 98304 | tf_op args[0]
  1.6 0.0 copy-done.2
  1.6 0.0 copy-start.1
  1.6 0.1 copy.8.cot_ref
  1.7 0.6 %copy-done.1 = s32[256]{0:T(256)S(1)} copy-done((s32[256]{0:T(256)S(1)}, s32[256]{0:T(256)}, u32[]{:S(2)}) %copy-start.1) | copy-done | bytes 1048
  2.3 0.0 copy-start
  2.3 1.1 %copy-done = bf16[27,96,96]{2,1,0:T(8,128)(2,1)S(1)} copy-done((bf16[27,96,96]{2,1,0:T(8,128)(2,1)S(1)}, bf16[27,96,96]{2,1,0:T(8,128)(2,1)}, u32[]{:S(2)}) %copy-start) | copy-done | bytes 497688
  3.4 46.6 %shard_map.67 = (bf16[256,96]{1,0:T(8,128)(2,1)S(1)}, bf16[256,96]{1,0:T(8,128)(2,1)S(1)}, f32[162,96]{1,0:T(8,128)S(1)}) custom-call(bf16[256,96]{1,0:T(8,128)(2,1)S(1)} %copy.7.feat_ref, bf16[256,96]{1,0:T(8,128)(2,1)S(1)} %copy.8.cot_ref, s32[1,256]{1,0:T(1,128)S(1)} %bitcast.1, bf16[27,96,96]{2,1,0:T(8,128)(2,1)S(1)} %copy-done), custom_call_target="tpu_custom_call" | custom-call | tf_op jit(solution)/shard_map/pallas_call | solution.py:348
  50.0 0.7 %copy.9 = bf16[256,96]{0,1:T(8,128)(2,1)} copy(bf16[256,96]{1,0:T(8,128)(2,1)S(1)} %get-tuple-element.9) | data formatting | bytes 98304
  50.7 0.7 %copy.10 = bf16[256,96]{0,1:T(8,128)(2,1)} copy(bf16[256,96]{1,0:T(8,128)(2,1)S(1)} %get-tuple-element.10) | data formatting | bytes 98304
  51.4 0.7 %reshape.13 = f32[15552]{0:T(1024)} reshape(f32[162,96]{1,0:T(8,128)S(1)} %get-tuple-element.8) | data formatting | bytes 124416 | tf_op jit(solution)/shard_map/reshape | solution.py:380
Async XLA Ops:
  0.6 0.9 %copy-start.2 = (bf16[256,96]{0,1:T(8,128)(2,1)S(1)}, bf16[256,96]{0,1:T(8,128)(2,1)}, u32[]{:S(2)}) copy-start(bf16[256,96]{0,1:T(8,128)(2,1)} %param.5) | copy-start | bytes 147460
  1.6 0.7 %copy-start.1 = (s32[256]{0:T(256)S(1)}, s32[256]{0:T(256)}, u32[]{:S(2)}) copy-start(s32[256]{0:T(256)} %param.6) | copy-start | bytes 3076
  2.3 1.1 %copy-start = (bf16[27,96,96]{2,1,0:T(8,128)(2,1)S(1)}, bf16[27,96,96]{2,1,0:T(8,128)(2,1)}, u32[]{:S(2)}) copy-start(bf16[27,96,96]{2,1,0:T(8,128)(2,1)} %weight_ref.1) | copy-start | bytes 1492996

commit v2 on v1

--- a/solution.py
+++ b/solution.py
@@ -64,12 +64,11 @@
         == lax.broadcasted_iota(jnp.int32, (rows, rows), 1)
     )
     eye = jnp.where(eye, 1.0, 0.0).astype(BF16)
-    column = lax.dot_general(eye, digits, (((1,), (1,)), ((), ())), preferred_element_type=F32)
+    spare = jnp.zeros((LANES - chan, rows), BF16)
+    lines_in = jnp.concatenate([feat_ref[...], digits[chan:LANES], cot_ref[...], spare], axis=0)
+    packed = lax.dot_general(eye, lines_in, (((1,), (1,)), ((), ())), preferred_element_type=F32)
     mine = number(w, n, s)
-    held[mine, 0:rows, 0:LANES] = column.astype(BF16)
-    held[mine, 0:rows, LANES : 2 * LANES] = jnp.zeros((rows, LANES), BF16)
-    held[mine, 0:rows, 0:chan] = feat_ref[...]
-    held[mine, 0:rows, LANES : LANES + chan] = cot_ref[...]
+    held[mine, 0:rows, :] = packed.astype(BF16)
     held[mine, rows : rows + 16, :] = digits[0:16]
 
     pl.semaphore_wait(barrier, owners)
@@ -105,84 +104,16 @@
     for t in range(27):
         taps[t, 0:chan, 0:chan] = weight_ref[t]
 
-    def crossed(distance):
-        def arrive(wi):
-            block = number(wi, 1 - n, s)
-            block_copy(block, 2, across).wait_recv()
-            block_copy(block, 3, sibling).start()
-
-        if distance == 0:
-            arrive(w)
-            return
-
-        @pl.when(w >= distance)
-        def _():
-            arrive(w - distance)
-
-        @pl.when(w + distance < wide_n)
-        def _():
-            arrive(w + distance)
-
-    for d in range(1, wide_n):
-
-        @pl.when(w >= d)
-        def _():
-            block = number(w - d, n, s)
-            block_copy(block, 0, up).wait_recv()
-
-            @pl.when(w + 1 < wide_n)
-            def _():
-                block_copy(block, 0, up).start()
-
-            block_copy(block, 2, across).start()
-            block_copy(block, 3, sibling).start()
-
-        @pl.when(w + d < wide_n)
-        def _():
-            block = number(w + d, n, s)
-            block_copy(block, 1, down).wait_recv()
-
-            @pl.when(w >= 1)
-            def _():
-                block_copy(block, 1, down).start()
-
-            block_copy(block, 2, across).start()
-            block_copy(block, 3, sibling).start()
-
-        crossed(d - 1)
-    crossed(wide_n - 1)
-
-    for o in range(owners):
-        block_copy(o * sub_n + 1 - s, 3, sibling).wait_recv()
-
-    for wi in range(wide_n):
-        block = number(wi, n, s)
-
-        @pl.when(jnp.logical_and(wi <= w, w + 1 < wide_n))
-        def _():
-            block_copy(block, 0, up).wait_send()
-
-        @pl.when(jnp.logical_and(wi >= w, w >= 1))
-        def _():
-            block_copy(block, 1, down).wait_send()
-
-        block_copy(block, 2, across).wait_send()
-        for ni in range(narrow_n):
-            block_copy(number(wi, ni, s), 3, sibling).wait_send()
-
     def slot_mask(block):
         lines = held[block, rows : rows + 16, :].astype(F32)
         slot_of = lines[0:1] * 16.0 + lines[1:2]
         order = lax.broadcasted_iota(jnp.int32, (slot_n, rows), 0).astype(F32)
         return jnp.where(order == slot_of, 1.0, 0.0).astype(BF16)
 
-    def to_slots(block, carry):
+    def to_slots(block):
         filled = jnp.dot(slot_mask(block), held[block, 0:rows, :], preferred_element_type=F32)
         source = block // sub_n
         slots[block % sub_n, :, source] = filled.astype(BF16).reshape(owners, cap, 2 * LANES)
-        return carry
-
-    lax.fori_loop(0, owners * sub_n, to_slots, 0)
 
     row_of = lax.broadcasted_iota(jnp.int32, (16, 2 * LANES), 0)
     lane_of = lax.broadcasted_iota(jnp.int32, (16, 2 * LANES), 1)
@@ -197,7 +128,7 @@
         order = lax.broadcasted_iota(jnp.int32, (cells, slot_n), 0).astype(F32) + 1.0
         return jnp.where(order == cell_of, 1.0, 0.0).astype(BF16), rows_in
 
-    def to_field(block, carry):
+    def to_field(block):
         ones, rows_in = cell_mask(block)
         dense = jnp.dot(ones, rows_in, preferred_element_type=F32)
         dense = dense.reshape(EDGE, half, EDGE, 2 * LANES)
@@ -209,9 +140,67 @@
         )
         x_field[at] = dense[..., 0:LANES]
         g_field[at] = dense[..., LANES : 2 * LANES]
+
+    to_slots(mine)
+
+    def offset(step):
+        distance = (step + 1) // 2
+        from_below = step % 2 == 1
+        wi = jnp.where(from_below, w - distance, w + distance)
+        return from_below, wi, jnp.logical_and(wi >= 0, wi < wide_n)
+
+    def arrive(step, carry):
+        from_below, wi, valid = offset(step)
+
+        @pl.when(jnp.logical_and(valid, jnp.logical_and(step >= 1, step < 2 * wide_n - 1)))
+        def _():
+            block = number(wi, n, s)
+            block_copy(block, 0, up).wait_recv()
+
+            @pl.when(jnp.logical_and(from_below, w + 1 < wide_n))
+            def _():
+                block_copy(block, 0, up).start()
+
+            @pl.when(jnp.logical_and(jnp.logical_not(from_below), w >= 1))
+            def _():
+                block_copy(block, 1, down).start()
+
+            block_copy(block, 2, across).start()
+            block_copy(block, 3, sibling).start()
+            to_slots(block)
+
+        _, wx, there = offset(step - 2)
+
+        @pl.when(jnp.logical_and(there, step >= 2))
+        def _():
+            block = number(wx, 1 - n, s)
+            block_copy(block, 2, across).wait_recv()
+            block_copy(block, 3, sibling).start()
+            to_slots(block)
+
         return carry
 
-    lax.fori_loop(0, owners * sub_n, to_field, 0)
+    lax.fori_loop(1, 2 * wide_n + 1, arrive, 0)
+
+    def fields_of(si, begin, end):
+        def one(i, carry):
+            wi = lax.rem(w + wide_n - 1 + i // narrow_n, wide_n)
+            to_field(number(wi, i % narrow_n, si))
+            return carry
+
+        lax.fori_loop(begin * narrow_n, end * narrow_n, one, 0)
+
+    close = min(3, wide_n)
+    fields_of(s, 0, close)
+
+    def from_sibling(o, carry):
+        block = o * sub_n + 1 - s
+        block_copy(block, 3, sibling).wait_recv()
+        to_slots(block)
+        return carry
+
+    lax.fori_loop(0, owners, from_sibling, 0)
+    fields_of(1 - s, 0, close)
     mask[...] = cell_mask(mine)[0]
 
     wide_at = pl.ds(pl.multiple_of(EDGE * w, EDGE), 3 * EDGE)
@@ -283,6 +272,8 @@
         reply_copy(delta).start()
     returned[me] = picked[me]
 
+    fields_of(s, close, wide_n)
+    fields_of(1 - s, close, wide_n)
     begin = mine * shard
     tap0 = begin // chan
     whole = EDGE * wide_n
@@ -325,12 +316,27 @@
     for delta in range(1, owners):
         reply_copy(delta).wait_send()
         reply_arrival(delta).wait_recv()
+    for wi in range(wide_n):
+        block = number(wi, n, s)
+
+        @pl.when(jnp.logical_and(wi <= w, w + 1 < wide_n))
+        def _():
+            block_copy(block, 0, up).wait_send()
+
+        @pl.when(jnp.logical_and(wi >= w, w >= 1))
+        def _():
+            block_copy(block, 1, down).wait_send()
+
+        block_copy(block, 2, across).wait_send()
+        for ni in range(narrow_n):
+            block_copy(number(wi, ni, s), 3, sibling).wait_send()
+
     answer = lax.dot_general(
-        slot_mask(mine), returned[...].reshape(slot_n, 2 * LANES), (((0,), (0,)), ((), ())),
+        returned[...].reshape(slot_n, 2 * LANES), slot_mask(mine), (((0,), (0,)), ((), ())),
         preferred_element_type=F32,
     ).astype(BF16)
-    out_ref[...] = answer[:, 0:chan]
-    grad_ref[...] = answer[:, LANES : LANES + chan]
+    out_ref[...] = answer[0:chan]
+    grad_ref[...] = answer[LANES : LANES + chan]
 
 
 def window_shards(features, cotangent, keys, weight):
@@ -348,8 +354,8 @@
     out, grad, terms = pl.pallas_call(
         functools.partial(window_kernel, dims),
         out_shape=(
-            jax.ShapeDtypeStruct((rows, chan), BF16),
-            jax.ShapeDtypeStruct((rows, chan), BF16),
+            jax.ShapeDtypeStruct((chan, rows), BF16),
+            jax.ShapeDtypeStruct((chan, rows), BF16),
             jax.ShapeDtypeStruct((shard, chan), F32),
         ),
         in_specs=[vmem] * 4,
@@ -376,8 +382,8 @@
         compiler_params=pltpu.CompilerParams(
             collective_id=0, has_side_effects=True, vmem_limit_bytes=50 * 1024 * 1024
         ),
-    )(features, cotangent, keys.reshape(1, rows), weight)
-    return out, grad, terms.reshape(-1)
+    )(features.T, cotangent.T, keys.reshape(1, rows), weight)
+    return out.T, grad.T, terms.reshape(-1)
 
 
 def extended(array, sides, width):

time: 52.4 us -> 53.1 us (1.013)
  no operation moved by 1% of the time
where the time goes in v2:
time: 53.1 us; the launch traced here: 52.9 us
  Pallas kernels  46.9 us (88%)
  local copies, waits for them, and re-layouts  5.32 us (10%)
  between operations  0.65 us (1%)
    pallas_call x1, Pallas kernels, window_shards(): pl.pallas_call(functools.partial(window_kernel, dims), out_shape=(jax.Sha...  46.9 us
    unnamed x10, local copies, waits for them, and re-layouts  4.6 us

profile of v2, /device:TPU:0, one launch (start us, length us, event | category | flops | bytes accessed | tf_op | source)
XLA Modules:
  0.0 52.9 jit_solution(16247124644857345091)
XLA Ops:
  0.6 0.0 copy-start.3
  0.6 0.7 %copy-done.3 = s32[256]{0:T(256)S(1)} copy-done((s32[256]{0:T(256)S(1)}, s32[256]{0:T(256)}, u32[]{:S(2)}) %copy-start.3) | copy-done | bytes 1048
  1.3 0.0 copy-start
  1.3 1.1 %copy-done = bf16[27,96,96]{2,1,0:T(8,128)(2,1)S(1)} copy-done((bf16[27,96,96]{2,1,0:T(8,128)(2,1)S(1)}, bf16[27,96,96]{2,1,0:T(8,128)(2,1)}, u32[]{:S(2)}) %copy-start) | copy-done | bytes 497688
  2.4 0.0 copy-start.1
  2.4 0.8 %copy-done.1 = bf16[256,96]{0,1:T(8,128)(2,1)S(1)} copy-done((bf16[256,96]{0,1:T(8,128)(2,1)S(1)}, bf16[256,96]{0,1:T(8,128)(2,1)}, u32[]{:S(2)}) %copy-start.1) | copy-done | bytes 49176
  3.2 0.0 copy-start.2
  3.2 0.8 %copy-done.2 = bf16[256,96]{0,1:T(8,128)(2,1)S(1)} copy-done((bf16[256,96]{0,1:T(8,128)(2,1)S(1)}, bf16[256,96]{0,1:T(8,128)(2,1)}, u32[]{:S(2)}) %copy-start.2) | copy-done | bytes 49176
  4.0 46.9 %shard_map.67 = (bf16[96,256]{1,0:T(8,128)(2,1)S(1)}, bf16[96,256]{1,0:T(8,128)(2,1)S(1)}, f32[162,96]{1,0:T(8,128)S(1)}) custom-call(bf16[96,256]{1,0:T(8,128)(2,1)S(1)} %bitcast.5, bf16[96,256]{1,0:T(8,128)(2,1)S(1)} %bitcast.6, s32[1,256]{1,0:T(1,128)S(1)} %bitcast.9, bf16[27,96,96]{2,1,0:T(8,128)(2,1)S(1)} %copy-done), custom_call_target="tpu_custom_call" | custom-call | tf_op jit(solution)/shard_map/pallas_call | solution.py:354
  50.9 0.7 %reshape.13 = f32[15552]{0:T(1024)} reshape(f32[162,96]{1,0:T(8,128)S(1)} %get-tuple-element.8) | data formatting | bytes 124416 | tf_op jit(solution)/shard_map/reshape | solution.py:386
  51.6 0.6 %copy.9 = bf16[256,96]{0,1:T(8,128)(2,1)} copy(bf16[256,96]{0,1:T(8,128)(2,1)S(1)} %bitcast.8) | data formatting | bytes 98304
  52.2 0.6 %copy.10 = bf16[256,96]{0,1:T(8,128)(2,1)} copy(bf16[256,96]{0,1:T(8,128)(2,1)S(1)} %bitcast.7) | data formatting | bytes 98304
Async XLA Ops:
  0.6 0.7 %copy-start.3 = (s32[256]{0:T(256)S(1)}, s32[256]{0:T(256)}, u32[]{:S(2)}) copy-start(s32[256]{0:T(256)} %param.6) | copy-start | bytes 3076
  1.3 1.1 %copy-start = (bf16[27,96,96]{2,1,0:T(8,128)(2,1)S(1)}, bf16[27,96,96]{2,1,0:T(8,128)(2,1)}, u32[]{:S(2)}) copy-start(bf16[27,96,96]{2,1,0:T(8,128)(2,1)} %weight_ref.1) | copy-start | bytes 1492996
  2.4 0.8 %copy-start.1 = (bf16[256,96]{0,1:T(8,128)(2,1)S(1)}, bf16[256,96]{0,1:T(8,128)(2,1)}, u32[]{:S(2)}) copy-start(bf16[256,96]{0,1:T(8,128)(2,1)} %param.4) | copy-start | bytes 147460
  3.2 0.8 %copy-start.2 = (bf16[256,96]{0,1:T(8,128)(2,1)S(1)}, bf16[256,96]{0,1:T(8,128)(2,1)}, u32[]{:S(2)}) copy-start(bf16[256,96]{0,1:T(8,128)(2,1)} %param.5) | copy-start | bytes 147460

commit v3 on v2

--- a/solution.py
+++ b/solution.py
@@ -14,9 +14,9 @@
 
 
 def window_kernel(
-    dims, feat_ref, cot_ref, keys_ref, weight_ref, out_ref, grad_ref, wgrad_ref,
+    dims, feat_in, cot_in, keys_in, weight_in, out_ref, grad_ref, wgrad_ref,
     held, slots, x_field, g_field, x_near, g_near, taps, mask, forward, backward,
-    picked, returned, terms, send_sem, recv_sem, reply_send, reply_recv,
+    picked, returned, terms, feat_ref, cot_ref, keys_ref, weight_ref, cell_rows, fetch_sem, send_sem, recv_sem, reply_send, reply_recv,
 ):
     wide_n, narrow_n, sub_n, rows, chan, cap, shard = dims
     owners = wide_n * narrow_n
@@ -32,6 +32,15 @@
     def place(wi, ni, si):
         return {"wide": wi, "narrow": ni, "sub": si}
 
+    fetches = [
+        pltpu.make_async_copy(source, goal, fetch_sem.at[i])
+        for i, (source, goal) in enumerate(
+            ((keys_in, keys_ref), (feat_in, feat_ref), (cot_in, cot_ref), (weight_in, weight_ref))
+        )
+    ]
+    for fetch in fetches:
+        fetch.start()
+
     barrier = pltpu.get_barrier_semaphore()
     for delta in range(1, owners):
         peer = lax.rem(me + delta, owners)
@@ -43,6 +52,7 @@
         barrier, inc=1, device_id=place(w, n, 1 - s), device_id_type=pl.DeviceIdType.MESH
     )
 
+    fetches[0].wait()
     keys = keys_ref[...]
     target = lax.shift_right_logical(keys, (cells * sub_n).bit_length() - 1)
     local = keys & (cells - 1)
@@ -64,6 +74,8 @@
         == lax.broadcasted_iota(jnp.int32, (rows, rows), 1)
     )
     eye = jnp.where(eye, 1.0, 0.0).astype(BF16)
+    fetches[1].wait()
+    fetches[2].wait()
     spare = jnp.zeros((LANES - chan, rows), BF16)
     lines_in = jnp.concatenate([feat_ref[...], digits[chan:LANES], cot_ref[...], spare], axis=0)
     packed = lax.dot_general(eye, lines_in, (((1,), (1,)), ((), ())), preferred_element_type=F32)
@@ -80,19 +92,26 @@
             device_id=target_place, device_id_type=pl.DeviceIdType.MESH,
         )
 
-    up, down = place(w + 1, n, s), place(w - 1, n, s)
     across, sibling = place(w, 1 - n, s), place(w, n, 1 - s)
-
-    @pl.when(w + 1 < wide_n)
-    def _():
-        block_copy(mine, 0, up).start()
-
-    @pl.when(w >= 1)
-    def _():
-        block_copy(mine, 1, down).start()
-
-    block_copy(mine, 2, across).start()
-    block_copy(mine, 3, sibling).start()
+    last, inner = wide_n - 1, wide_n
+
+    def along(distance, above):
+        peer = w + distance if above else w - distance
+        kind = lax.rem(peer - w + wide_n, wide_n) - 1
+        return block_copy(mine, kind, place(peer, n, s))
+
+    block_copy(mine, last, across).start()
+    for distance in range(1, wide_n):
+
+        @pl.when(w + distance < wide_n)
+        def _():
+            along(distance, True).start()
+
+        @pl.when(w >= distance)
+        def _():
+            along(distance, False).start()
+
+    block_copy(mine, inner, sibling).start()
 
     def clear(i, carry):
         x_field[i] = jnp.zeros(x_field.shape[1:], F32)
@@ -101,6 +120,7 @@
 
     lax.fori_loop(0, x_field.shape[0], clear, 0)
     taps[...] = jnp.zeros(taps.shape, BF16)
+    fetches[3].wait()
     for t in range(27):
         taps[t, 0:chan, 0:chan] = weight_ref[t]
 
@@ -120,17 +140,22 @@
     chooser = jnp.where(lane_of == chan, 16.0, jnp.where(lane_of == chan + 1, 1.0, 0.0))
     chooser = jnp.where(row_of == 0, chooser, 0.0).astype(BF16)
 
+    def find_cells(si):
+        found = lax.dot_general(
+            chooser, slots[si].reshape(owners * slot_n, 2 * LANES), (((1,), (1,)), ((), ())),
+            preferred_element_type=F32,
+        )
+        for o in range(owners):
+            cell_rows[si, o] = found[0:8, o * slot_n : (o + 1) * slot_n]
+
     def cell_mask(block):
+        cell_of = cell_rows[block % sub_n, block // sub_n][0:1]
+        order = lax.broadcasted_iota(jnp.int32, (cells, slot_n), 0).astype(F32) + 1.0
+        return jnp.where(order == cell_of, 1.0, 0.0).astype(BF16)
+
+    def to_field(block):
         rows_in = slots[block % sub_n, block // sub_n].reshape(slot_n, 2 * LANES)
-        cell_of = lax.dot_general(
-            chooser, rows_in, (((1,), (1,)), ((), ())), preferred_element_type=F32
-        )[0:1]
-        order = lax.broadcasted_iota(jnp.int32, (cells, slot_n), 0).astype(F32) + 1.0
-        return jnp.where(order == cell_of, 1.0, 0.0).astype(BF16), rows_in
-
-    def to_field(block):
-        ones, rows_in = cell_mask(block)
-        dense = jnp.dot(ones, rows_in, preferred_element_type=F32)
+        dense = jnp.dot(cell_mask(block), rows_in, preferred_element_type=F32)
         dense = dense.reshape(EDGE, half, EDGE, 2 * LANES)
         owner = block // sub_n
         at = (
@@ -145,37 +170,27 @@
 
     def offset(step):
         distance = (step + 1) // 2
-        from_below = step % 2 == 1
-        wi = jnp.where(from_below, w - distance, w + distance)
-        return from_below, wi, jnp.logical_and(wi >= 0, wi < wide_n)
+        wi = jnp.where(step % 2 == 1, w - distance, w + distance)
+        return wi, jnp.logical_and(wi >= 0, wi < wide_n)
 
     def arrive(step, carry):
-        from_below, wi, valid = offset(step)
+        wi, valid = offset(step)
 
         @pl.when(jnp.logical_and(valid, jnp.logical_and(step >= 1, step < 2 * wide_n - 1)))
         def _():
             block = number(wi, n, s)
-            block_copy(block, 0, up).wait_recv()
-
-            @pl.when(jnp.logical_and(from_below, w + 1 < wide_n))
-            def _():
-                block_copy(block, 0, up).start()
-
-            @pl.when(jnp.logical_and(jnp.logical_not(from_below), w >= 1))
-            def _():
-                block_copy(block, 1, down).start()
-
-            block_copy(block, 2, across).start()
-            block_copy(block, 3, sibling).start()
+            block_copy(block, last, across).wait_recv()
+            block_copy(block, last, across).start()
+            block_copy(block, inner, sibling).start()
             to_slots(block)
 
-        _, wx, there = offset(step - 2)
+        wx, there = offset(step - 2)
 
         @pl.when(jnp.logical_and(there, step >= 2))
         def _():
             block = number(wx, 1 - n, s)
-            block_copy(block, 2, across).wait_recv()
-            block_copy(block, 3, sibling).start()
+            block_copy(block, last, across).wait_recv()
+            block_copy(block, inner, sibling).start()
             to_slots(block)
 
         return carry
@@ -188,20 +203,22 @@
             to_field(number(wi, i % narrow_n, si))
             return carry
 
-        lax.fori_loop(begin * narrow_n, end * narrow_n, one, 0)
+        lax.fori_loop(begin * narrow_n, end * narrow_n, one, 0, unroll=2)
 
     close = min(3, wide_n)
+    find_cells(s)
     fields_of(s, 0, close)
 
     def from_sibling(o, carry):
         block = o * sub_n + 1 - s
-        block_copy(block, 3, sibling).wait_recv()
+        block_copy(block, inner, sibling).wait_recv()
         to_slots(block)
         return carry
 
     lax.fori_loop(0, owners, from_sibling, 0)
+    find_cells(1 - s)
     fields_of(1 - s, 0, close)
-    mask[...] = cell_mask(mine)[0]
+    mask[...] = cell_mask(mine)
 
     wide_at = pl.ds(pl.multiple_of(EDGE * w, EDGE), 3 * EDGE)
 
@@ -316,20 +333,13 @@
     for delta in range(1, owners):
         reply_copy(delta).wait_send()
         reply_arrival(delta).wait_recv()
+    for delta in range(1, wide_n):
+        block_copy(mine, delta - 1, across).wait_send()
     for wi in range(wide_n):
         block = number(wi, n, s)
-
-        @pl.when(jnp.logical_and(wi <= w, w + 1 < wide_n))
-        def _():
-            block_copy(block, 0, up).wait_send()
-
-        @pl.when(jnp.logical_and(wi >= w, w >= 1))
-        def _():
-            block_copy(block, 1, down).wait_send()
-
-        block_copy(block, 2, across).wait_send()
+        block_copy(block, last, across).wait_send()
         for ni in range(narrow_n):
-            block_copy(number(wi, ni, s), 3, sibling).wait_send()
+            block_copy(number(wi, ni, s), inner, sibling).wait_send()
 
     answer = lax.dot_general(
         returned[...].reshape(slot_n, 2 * LANES), slot_mask(mine), (((0,), (0,)), ((), ())),
@@ -358,7 +368,7 @@
             jax.ShapeDtypeStruct((chan, rows), BF16),
             jax.ShapeDtypeStruct((shard, chan), F32),
         ),
-        in_specs=[vmem] * 4,
+        in_specs=[pl.BlockSpec(memory_space=pltpu.HBM)] * 4,
         out_specs=(vmem,) * 3,
         scratch_shapes=[
             pltpu.VMEM((owners * sub_n, rows + 16, 2 * LANES), BF16),
@@ -374,13 +384,19 @@
             pltpu.VMEM((owners, cap, 2 * LANES), BF16),
             pltpu.VMEM((owners, cap, 2 * LANES), BF16),
             pltpu.VMEM((LANES, 3 * LANES), F32),
-            pltpu.SemaphoreType.DMA((owners * sub_n, 4)),
+            pltpu.VMEM((chan, rows), BF16),
+            pltpu.VMEM((chan, rows), BF16),
+            pltpu.VMEM((1, rows), jnp.int32),
+            pltpu.VMEM((27, chan, chan), BF16),
+            pltpu.VMEM((sub_n, owners, 8, owners * cap), F32),
+            pltpu.SemaphoreType.DMA((4,)),
+            pltpu.SemaphoreType.DMA((owners * sub_n, wide_n + 1)),
             pltpu.SemaphoreType.DMA((owners * sub_n,)),
             pltpu.SemaphoreType.DMA((owners,)),
             pltpu.SemaphoreType.DMA((owners,)),
         ],
         compiler_params=pltpu.CompilerParams(
-            collective_id=0, has_side_effects=True, vmem_limit_bytes=50 * 1024 * 1024
+            collective_id=0, has_side_effects=True, vmem_limit_bytes=63 * 1024 * 1024
         ),
     )(features.T, cotangent.T, keys.reshape(1, rows), weight)
     return out.T, grad.T, terms.reshape(-1)

time: 53.1 us -> 50 us (0.942)
  local copies, waits for them, and re-layouts: 5.32 us -> 3.07 us
  Pallas kernels: 46.9 us -> 46 us
    unnamed x10 -> x6, local copies, waits for them, and re-layouts: 4.6 us -> 1.44 us
    reshape x1, local copies, waits for them, and re-layouts: 0.73 us -> 1.63 us  [window_shards(): return (out.T, grad.T, terms.reshape(-1))]
    pallas_call x1, Pallas kernels: 46.9 us -> 46 us  [window_shards(): pl.pallas_call(functools.partial(window_kernel, dims), out_shape=(jax.Sha...]
where the time goes in v3:
time: 50 us; the launch traced here: 49.7 us
  Pallas kernels  46 us (92%)
  local copies, waits for them, and re-layouts  3.07 us (6%)
  between operations  0.65 us (1%)
    pallas_call x1, Pallas kernels, window_shards(): pl.pallas_call(functools.partial(window_kernel, dims), out_shape=(jax.Sha...  46 us
    reshape x1, local copies, waits for them, and re-layouts, window_shards(): return (out.T, grad.T, terms.reshape(-1))  1.63 us
    unnamed x6, local copies, waits for them, and re-layouts  1.44 us

profile of v3, /device:TPU:0, one launch (start us, length us, event | category | flops | bytes accessed | tf_op | source)
XLA Modules:
  0.0 49.7 jit_solution(12333033820610380021)
XLA Ops:
  0.6 46.0 %shard_map.67 = (bf16[96,256]{1,0:T(8,128)(2,1)}, bf16[96,256]{1,0:T(8,128)(2,1)}, f32[162,96]{1,0:T(8,128)}) custom-call(bf16[96,256]{1,0:T(8,128)(2,1)} %bitcast.5, bf16[96,256]{1,0:T(8,128)(2,1)} %bitcast.6, s32[1,256]{1,0:T(1,128)} %bitcast.9, bf16[27,96,96]{2,1,0:T(8,128)(2,1)} %weight_in.1), custom_call_target="tpu_custom_call" | custom-call | tf_op jit(solution)/shard_map/pallas_call | solution.py:364
  46.7 0.0 copy-start.1
  46.7 1.6 %reshape.13 = f32[15552]{0:T(1024)} reshape(f32[162,96]{1,0:T(8,128)} %get-tuple-element.8) | data formatting | bytes 124416 | tf_op jit(solution)/shard_map/reshape | solution.py:402
  48.3 0.0 copy-done.1
  48.3 0.0 copy-start
  48.3 0.6 %copy.9 = bf16[256,96]{0,1:T(8,128)(2,1)} copy(bf16[256,96]{0,1:T(8,128)(2,1)S(1)} %bitcast.8) | data formatting | bytes 98304
  48.9 0.2 copy-done
  49.1 0.6 %copy.10 = bf16[256,96]{0,1:T(8,128)(2,1)} copy(bf16[256,96]{0,1:T(8,128)(2,1)S(1)} %bitcast.7) | data formatting | bytes 98304
Async XLA Ops:
  46.7 1.6 %copy-start.1 = (bf16[96,256]{1,0:T(8,128)(2,1)S(1)}, bf16[96,256]{1,0:T(8,128)(2,1)}, u32[]{:S(2)}) copy-start(bf16[96,256]{1,0:T(8,128)(2,1)} %get-tuple-element.6) | copy-start | bytes 147460
  48.3 0.8 %copy-start = (bf16[96,256]{1,0:T(8,128)(2,1)S(1)}, bf16[96,256]{1,0:T(8,128)(2,1)}, u32[]{:S(2)}) copy-start(bf16[96,256]{1,0:T(8,128)(2,1)} %get-tuple-element.7) | copy-start | bytes 147460

commit v4 on v3

--- a/solution.py
+++ b/solution.py
@@ -63,25 +63,18 @@
         first = jnp.where(target == o, before, first)
     slot = target * cap + lax.broadcasted_iota(jnp.int32, keys.shape, 1) - first
     cell1 = cell + 1
-    line = lax.broadcasted_iota(jnp.int32, (LANES, rows), 0)
+    line = lax.broadcasted_iota(jnp.int32, (16, rows), 0)
     digits = jnp.where(line == 0, slot >> 4, 0)
     digits = jnp.where(line == 1, slot & 15, digits)
-    digits = jnp.where(line == chan, cell1 >> 4, digits)
-    digits = jnp.where(line == chan + 1, cell1 & 15, digits)
+    digits = jnp.where(line == 2, cell1 >> 4, digits)
+    digits = jnp.where(line == 3, cell1 & 15, digits)
     digits = digits.astype(F32).astype(BF16)
-    eye = (
-        lax.broadcasted_iota(jnp.int32, (rows, rows), 0)
-        == lax.broadcasted_iota(jnp.int32, (rows, rows), 1)
-    )
-    eye = jnp.where(eye, 1.0, 0.0).astype(BF16)
     fetches[1].wait()
     fetches[2].wait()
-    spare = jnp.zeros((LANES - chan, rows), BF16)
-    lines_in = jnp.concatenate([feat_ref[...], digits[chan:LANES], cot_ref[...], spare], axis=0)
-    packed = lax.dot_general(eye, lines_in, (((1,), (1,)), ((), ())), preferred_element_type=F32)
     mine = number(w, n, s)
-    held[mine, 0:rows, :] = packed.astype(BF16)
-    held[mine, rows : rows + 16, :] = digits[0:16]
+    held[mine, 0:chan, :] = feat_ref[...]
+    held[mine, chan : chan + 16, :] = digits
+    held[mine, chan + 16 : 2 * chan + 16, :] = cot_ref[...]
 
     pl.semaphore_wait(barrier, owners)
 
@@ -125,19 +118,29 @@
         taps[t, 0:chan, 0:chan] = weight_ref[t]
 
     def slot_mask(block):
-        lines = held[block, rows : rows + 16, :].astype(F32)
+        lines = held[block, chan : chan + 16, :].astype(F32)
         slot_of = lines[0:1] * 16.0 + lines[1:2]
         order = lax.broadcasted_iota(jnp.int32, (slot_n, rows), 0).astype(F32)
         return jnp.where(order == slot_of, 1.0, 0.0).astype(BF16)
 
     def to_slots(block):
-        filled = jnp.dot(slot_mask(block), held[block, 0:rows, :], preferred_element_type=F32)
+        spare = jnp.zeros((LANES - chan, rows), BF16)
+        lines_in = jnp.concatenate(
+            [
+                held[block, 0 : chan + 16, :], spare[16:],
+                held[block, chan + 16 : 2 * chan + 16, :], spare,
+            ],
+            axis=0,
+        )
+        filled = lax.dot_general(
+            slot_mask(block), lines_in, (((1,), (1,)), ((), ())), preferred_element_type=F32
+        )
         source = block // sub_n
         slots[block % sub_n, :, source] = filled.astype(BF16).reshape(owners, cap, 2 * LANES)
 
     row_of = lax.broadcasted_iota(jnp.int32, (16, 2 * LANES), 0)
     lane_of = lax.broadcasted_iota(jnp.int32, (16, 2 * LANES), 1)
-    chooser = jnp.where(lane_of == chan, 16.0, jnp.where(lane_of == chan + 1, 1.0, 0.0))
+    chooser = jnp.where(lane_of == chan + 2, 16.0, jnp.where(lane_of == chan + 3, 1.0, 0.0))
     chooser = jnp.where(row_of == 0, chooser, 0.0).astype(BF16)
 
     def find_cells(si):
@@ -371,7 +374,7 @@
         in_specs=[pl.BlockSpec(memory_space=pltpu.HBM)] * 4,
         out_specs=(vmem,) * 3,
         scratch_shapes=[
-            pltpu.VMEM((owners * sub_n, rows + 16, 2 * LANES), BF16),
+            pltpu.VMEM((owners * sub_n, 2 * chan + 16, rows), BF16),
             pltpu.VMEM((sub_n, owners, owners, cap, 2 * LANES), BF16),
             pltpu.VMEM(field, F32),
             pltpu.VMEM(field, F32),

time: 50 us -> 45.7 us (0.914)
  Pallas kernels: 46 us -> 41.7 us
    pallas_call x1, Pallas kernels: 46 us -> 41.7 us  [window_shards(): pl.pallas_call(functools.partial(window_kernel, dims), out_shape=(jax.Sha...]
where the time goes in v4:
time: 45.7 us; the launch traced here: 45.5 us
  Pallas kernels  41.7 us (91%)
  local copies, waits for them, and re-layouts  3.07 us (7%)
  between operations  0.65 us (1%)
    pallas_call x1, Pallas kernels, window_shards(): pl.pallas_call(functools.partial(window_kernel, dims), out_shape=(jax.Sha...  41.7 us
    reshape x1, local copies, waits for them, and re-layouts, window_shards(): return (out.T, grad.T, terms.reshape(-1))  1.63 us
    unnamed x6, local copies, waits for them, and re-layouts  1.44 us

profile of v4, /device:TPU:0, one launch (start us, length us, event | category | flops | bytes accessed | tf_op | source)
XLA Modules:
  0.0 45.5 jit_solution(7383960004307878339)
XLA Ops:
  0.6 41.7 %shard_map.67 = (bf16[96,256]{1,0:T(8,128)(2,1)}, bf16[96,256]{1,0:T(8,128)(2,1)}, f32[162,96]{1,0:T(8,128)}) custom-call(bf16[96,256]{1,0:T(8,128)(2,1)} %bitcast.5, bf16[96,256]{1,0:T(8,128)(2,1)} %bitcast.6, s32[1,256]{1,0:T(1,128)} %bitcast.9, bf16[27,96,96]{2,1,0:T(8,128)(2,1)} %weight_in.1), custom_call_target="tpu_custom_call" | custom-call | tf_op jit(solution)/shard_map/pallas_call | solution.py:367
  42.4 0.0 copy-start.1
  42.4 1.6 %reshape.13 = f32[15552]{0:T(1024)} reshape(f32[162,96]{1,0:T(8,128)} %get-tuple-element.8) | data formatting | bytes 124416 | tf_op jit(solution)/shard_map/reshape | solution.py:405
  44.0 0.0 copy-done.1
  44.0 0.0 copy-start
  44.0 0.6 %copy.9 = bf16[256,96]{0,1:T(8,128)(2,1)} copy(bf16[256,96]{0,1:T(8,128)(2,1)S(1)} %bitcast.8) | data formatting | bytes 98304
  44.6 0.2 copy-done
  44.8 0.6 %copy.10 = bf16[256,96]{0,1:T(8,128)(2,1)} copy(bf16[256,96]{0,1:T(8,128)(2,1)S(1)} %bitcast.7) | data formatting | bytes 98304
Async XLA Ops:
  42.4 1.6 %copy-start.1 = (bf16[96,256]{1,0:T(8,128)(2,1)S(1)}, bf16[96,256]{1,0:T(8,128)(2,1)}, u32[]{:S(2)}) copy-start(bf16[96,256]{1,0:T(8,128)(2,1)} %get-tuple-element.6) | copy-start | bytes 147460
  44.0 0.8 %copy-start = (bf16[96,256]{1,0:T(8,128)(2,1)S(1)}, bf16[96,256]{1,0:T(8,128)(2,1)}, u32[]{:S(2)}) copy-start(bf16[96,256]{1,0:T(8,128)(2,1)} %get-tuple-element.7) | copy-start | bytes 147460

commit v5 on v4

--- a/solution.py
+++ b/solution.py
@@ -206,7 +206,7 @@
             to_field(number(wi, i % narrow_n, si))
             return carry
 
-        lax.fori_loop(begin * narrow_n, end * narrow_n, one, 0, unroll=2)
+        lax.fori_loop(begin * narrow_n, end * narrow_n, one, 0, unroll=True)
 
     close = min(3, wide_n)
     find_cells(s)
@@ -218,7 +218,7 @@
         to_slots(block)
         return carry
 
-    lax.fori_loop(0, owners, from_sibling, 0)
+    lax.fori_loop(0, owners, from_sibling, 0, unroll=2)
     find_cells(1 - s)
     fields_of(1 - s, 0, close)
     mask[...] = cell_mask(mine)
@@ -235,7 +235,7 @@
                 g_near[j, i, k] = g_line[begin : begin + EDGE].astype(BF16)
         return carry
 
-    lax.fori_loop(0, EDGE + 2, near, 0)
+    lax.fori_loop(0, EDGE + 2, near, 0, unroll=3)
 
     forward[...] = jnp.zeros(forward.shape, F32)
     backward[...] = jnp.zeros(backward.shape, F32)
@@ -262,7 +262,7 @@
         backward[...] = total
         return carry
 
-    lax.fori_loop(0, 9, conv, 0)
+    lax.fori_loop(0, 9, conv, 0, unroll=3)
 
     reply = jnp.concatenate([forward[...].astype(BF16), backward[...].astype(BF16)], axis=1)
     rows_out = lax.dot_general(
@@ -325,7 +325,7 @@
         )
         return carry
 
-    lax.fori_loop(0, EDGE * narrow_n, gather, 0)
+    lax.fori_loop(0, EDGE * narrow_n, gather, 0, unroll=4)
     total_rows = rows * owners * sub_n
     factor = F32(1.0) / jnp.sqrt(F32(total_rows))
     for m in range(3):

time: 45.7 us -> 42.5 us (0.930)
  Pallas kernels: 41.7 us -> 38.5 us
    pallas_call x1, Pallas kernels: 41.7 us -> 38.5 us  [window_shards(): pl.pallas_call(functools.partial(window_kernel, dims), out_shape=(jax.Sha...]
where the time goes in v5:
time: 42.5 us; the launch traced here: 42.2 us
  Pallas kernels  38.5 us (91%)
  local copies, waits for them, and re-layouts  3.07 us (7%)
  between operations  0.65 us (2%)
    pallas_call x1, Pallas kernels, window_shards(): pl.pallas_call(functools.partial(window_kernel, dims), out_shape=(jax.Sha...  38.5 us
    reshape x1, local copies, waits for them, and re-layouts, window_shards(): return (out.T, grad.T, terms.reshape(-1))  1.63 us
    unnamed x6, local copies, waits for them, and re-layouts  1.44 us

profile of v5, /device:TPU:0, one launch (start us, length us, event | category | flops | bytes accessed | tf_op | source)
XLA Modules:
  0.0 42.2 jit_solution(10854991943445187439)
XLA Ops:
  0.6 38.5 %shard_map.67 = (bf16[96,256]{1,0:T(8,128)(2,1)}, bf16[96,256]{1,0:T(8,128)(2,1)}, f32[162,96]{1,0:T(8,128)}) custom-call(bf16[96,256]{1,0:T(8,128)(2,1)} %bitcast.5, bf16[96,256]{1,0:T(8,128)(2,1)} %bitcast.6, s32[1,256]{1,0:T(1,128)} %bitcast.9, bf16[27,96,96]{2,1,0:T(8,128)(2,1)} %weight_in.1), custom_call_target="tpu_custom_call" | custom-call | tf_op jit(solution)/shard_map/pallas_call | solution.py:367
  39.2 0.0 copy-start.1
  39.2 1.6 %reshape.13 = f32[15552]{0:T(1024)} reshape(f32[162,96]{1,0:T(8,128)} %get-tuple-element.8) | data formatting | bytes 124416 | tf_op jit(solution)/shard_map/reshape | solution.py:405
  40.8 0.0 copy-done.1
  40.8 0.0 copy-start
  40.8 0.6 %copy.9 = bf16[256,96]{0,1:T(8,128)(2,1)} copy(bf16[256,96]{0,1:T(8,128)(2,1)S(1)} %bitcast.8) | data formatting | bytes 98304
  41.4 0.2 copy-done
  41.6 0.6 %copy.10 = bf16[256,96]{0,1:T(8,128)(2,1)} copy(bf16[256,96]{0,1:T(8,128)(2,1)S(1)} %bitcast.7) | data formatting | bytes 98304
Async XLA Ops:
  39.2 1.6 %copy-start.1 = (bf16[96,256]{1,0:T(8,128)(2,1)S(1)}, bf16[96,256]{1,0:T(8,128)(2,1)}, u32[]{:S(2)}) copy-start(bf16[96,256]{1,0:T(8,128)(2,1)} %get-tuple-element.6) | copy-start | bytes 147460
  40.8 0.8 %copy-start = (bf16[96,256]{1,0:T(8,128)(2,1)S(1)}, bf16[96,256]{1,0:T(8,128)(2,1)}, u32[]{:S(2)}) copy-start(bf16[96,256]{1,0:T(8,128)(2,1)} %get-tuple-element.7) | copy-start | bytes 147460
